TPU v7x, 32 devices: a whole 2x2x4 slice. The times are simulated.
32 devices in a mesh: dp: 8 (over z, x), tensor: 4 (over y, core).
Axes of the slice: x: 2, y: 2, z: 4, core: 2. Of those that a mesh axis runs over, the one named last changes fastest.
Arguments:
- tokens: bfloat16 [4096, 2048], P('dp'), may hold values from -6 to 6
- norm_attn: float32 [2048], replicated, may hold values from 0.5 to 1.5
- w_query: bfloat16 [2048, 2048], P(None, 'tensor'), may hold values from -0.125 to 0.125
- key_weight: bfloat16 [2048, 1024], P(None, 'tensor'), may hold values from -0.125 to 0.125
- value_weight: bfloat16 [2048, 1024], P(None, 'tensor'), may hold values from -0.125 to 0.125
- query_gain: float32 [128], replicated, may hold values from 0.5 to 1.5
- key_gain: float32 [128], replicated, may hold values from 0.5 to 1.5
- w_out: bfloat16 [2048, 2048], P('tensor'), may hold values from -2 to 2
- norm_mlp: float32 [2048], replicated, may hold values from 0.5 to 1.5
- w_gate: bfloat16 [2048, 6144], P(None, 'tensor'), may hold values from -0.125 to 0.125
- w_up: bfloat16 [2048, 6144], P(None, 'tensor'), may hold values from -0.125 to 0.125
- w_down: bfloat16 [6144, 2048], P('tensor'), may hold values from -0.078125 to 0.078125
- out_grad: bfloat16 [4096, 2048], P('dp'), may hold values from -6 to 6
- prefix_len: int32 [1], replicated, may hold values from 409 to 2048
Outputs:
- block_out: bfloat16 [4096, 2048], P('dp')
- tokens_grad: float32 [4096, 2048], P('dp')
- norm_attn_grad: float32 [2048], P('dp')
- w_query_grad: float32 [2048, 2048], P('dp', 'tensor')
- w_key_grad: float32 [2048, 1024], P('dp', 'tensor')
- w_value_grad: float32 [2048, 1024], P('dp', 'tensor')
- query_gain_grad: float32 [128], replicated
- key_gain_grad: float32 [128], replicated
- w_out_grad: float32 [2048, 2048], P('tensor', 'dp')
- norm_mlp_grad: float32 [2048], P('dp')
- w_gate_grad: float32 [2048, 6144], P('dp', 'tensor')
- w_up_grad: float32 [2048, 6144], P('dp', 'tensor')
- w_down_grad: float32 [6144, 2048], P('tensor', 'dp')
Inputs may be any that keep to these rules, and one draw needn't show every extreme that they name: `prefix_len`: leading tokens of each sequence that see one another in both directions.
All inputs are finite; a program needn't handle non-finite values.
Results may differ from a plain program's by a relative error of at most 0.024.
Values may be sent and summed in bfloat16 or wider, within the bound.
A program may use at most 256 MiB of HBM per device.

v0:
```python
import functools
import math

import jax
import jax.numpy as jnp
from jax import lax
from jax.experimental import pallas as pl
from jax.experimental.pallas import tpu as pltpu
from jax.sharding import PartitionSpec as P

F32 = jnp.float32
BF16 = jnp.bfloat16
EPS = 1e-06
ROPE_BASE = 1000000.0
MAX_PREFIX = 2048
VMEM_LIMIT = 56 * 2**20
BACK_VMEM_LIMIT = 60 * 2**20

COST = pl.CostEstimate(flops=1000, bytes_accessed=1000, transcendentals=0)

NN = (((1,), (0,)), ((), ()))
NT = (((1,), (1,)), ((), ()))
TN = (((0,), (0,)), ((), ()))


def dot(left, right, dims=NN):
    return lax.dot_general(left, right, dims, preferred_element_type=F32)


def vmem(count):
    return [pl.BlockSpec(memory_space=pltpu.VMEM)] * count


def params():
    return pltpu.CompilerParams(vmem_limit_bytes=VMEM_LIMIT)


def greet(peers):
    barrier = pltpu.get_barrier_semaphore()
    count = 0
    for peer, there in peers:

        def signal(peer=peer):
            pl.semaphore_signal(barrier, 1, device_id=peer, device_id_type=pl.DeviceIdType.MESH)

        if there is True:
            signal()
            count = count + 1
        else:
            pl.when(there)(signal)
            count = count + there.astype(jnp.int32)
    pl.semaphore_wait(barrier, count)


def remote(src, dst, send, recv, peer):
    return pltpu.make_async_remote_copy(
        src_ref=src,
        dst_ref=dst,
        send_sem=send,
        recv_sem=recv,
        device_id=peer,
        device_id_type=pl.DeviceIdType.MESH,
    )


class Staged:
    def __init__(self, arrays, buffers, sems, out=False):
        self.copies = []
        for i, (array, buffer) in enumerate(zip(arrays, buffers)):
            ends = (buffer, array) if out else (array, buffer)
            self.copies.append((buffer, pltpu.make_async_copy(*ends, sems.at[i])))

    @staticmethod
    def scratch(shapes):
        return [pltpu.VMEM(s.shape, s.dtype) for s in shapes] + [pltpu.SemaphoreType.DMA((len(shapes),))]

    def start(self, *buffers):
        for buffer, copy in self.copies:
            if not buffers or any(buffer is b for b in buffers):
                copy.start()

    def wait(self, *buffers):
        for buffer, copy in self.copies:
            if not buffers or any(buffer is b for b in buffers):
                copy.wait()


ANYWHERE = pl.BlockSpec(memory_space=pl.ANY)


def tensor_peers():
    t = lax.axis_index("tensor")
    core = t % 2
    y = t // 2
    return core, {"tensor": t + 1 - 2 * core}, {"tensor": t + 2 - 4 * y}


def rows_of(core, half):
    return pl.ds(pl.multiple_of(core * half, half), half)


def cut_into(out, out_rows, ref, ref_rows, side, planes, shard):
    for z in range(planes):
        to = slice(z * shard, (z + 1) * shard)
        if shard % 128 == 0:
            at = pl.ds(pl.multiple_of((2 * z + side) * shard, shard), shard)
            out[out_rows, to] = ref[ref_rows, at]
        else:
            low = ref[ref_rows, 2 * z * shard : (2 * z + 1) * shard]
            high = ref[ref_rows, (2 * z + 1) * shard : (2 * z + 2) * shard]
            out[out_rows, to] = jnp.where(side == 0, low, high)


class Columns:
    def __init__(self, whole, keep, came, scratch, x_at, core, x_peer, core_peer, planes, shard):
        self.whole, self.keep, self.came = whole, keep, came
        self.send_ref, self.recv_ref, self.sems = scratch[0], scratch[1], scratch[2:]
        self.x_at, self.core, self.cut = x_at, core, (planes, shard)
        self.x_peer, self.core_peer = x_peer, core_peer
        self.half = whole.shape[0] // 2

    @staticmethod
    def scratch(half, columns):
        return [pltpu.VMEM((half, columns), BF16)] * 2 + [pltpu.SemaphoreType.DMA] * 4

    def over_x(self):
        return remote(self.send_ref, self.recv_ref, self.sems[0], self.sems[1], self.x_peer)

    def over_core(self):
        there = self.came.at[rows_of(self.core, self.half), :]
        return remote(self.recv_ref, there, self.sems[2], self.sems[3], self.core_peer)

    def start(self):
        mine = rows_of(self.core, self.half)
        cut_into(self.send_ref, slice(None), self.whole, mine, 1 - self.x_at, *self.cut)
        self.over_x().start()

    def store(self):
        cut_into(self.keep, slice(None), self.whole, slice(None), self.x_at, *self.cut)

    def forward(self):
        self.over_x().wait_recv()
        self.over_core().start()
        self.came[rows_of(self.core, self.half), :] = self.recv_ref[...]

    def finish(self):
        self.over_core().wait_recv()
        self.over_x().wait_send()
        self.over_core().wait_send()


class LineSum:
    def __init__(self, scratch, device, plane, planes, paced=False):
        self.paced = paced
        self.stack, self.came = scratch[:2]
        self.sems = scratch[2:]
        self.device, self.plane, self.planes = device, plane, planes

    @staticmethod
    def scratch(planes, shape):
        return [pltpu.VMEM((n,) + shape, BF16) for n in (planes, planes + 1)] + [
            pltpu.SemaphoreType.DMA((planes,))
        ] * 4

    def up(self, j):
        s = self.sems
        peer = {"dp": self.device + 2}
        return remote(self.stack.at[j], self.came.at[j], s[0].at[j], s[1].at[j], peer)

    def down(self, j):
        s = self.sems
        slot = jnp.where(self.plane - 1 == j, self.planes, j)
        peer = {"dp": self.device - 2}
        return remote(self.stack.at[j], self.came.at[slot], s[2].at[j], s[3].at[j], peer)

    def start(self):
        last = self.planes - 1

        @pl.when(self.plane == 0)
        def _():
            for j in range(last, last - 1 if self.paced else 0, -1):
                self.up(j).start()

        @pl.when(self.plane == last)
        def _():
            for j in range(1 if self.paced else last):
                self.down(j).start()

    def advance(self, step):
        plane, last = self.plane, self.planes - 1
        low, high = last - step + plane, step - last + plane
        if self.paced:

            @pl.when(plane == 0)
            def _():
                self.up(last - step + 1).wait_send()
                self.up(last - step).start()

            @pl.when(plane == last)
            def _():
                self.down(step - 1).wait_send()
                self.down(step).start()

        @pl.when((plane >= 1) & (plane <= step))
        def _():
            self.up(low).wait_recv()
            self.stack[low] += self.came[low]
            self.up(low).start()

        @pl.when((plane < last) & (plane >= last - step))
        def _():
            self.down(high).wait_recv()
            self.stack[high] += self.came[high]
            self.down(high).start()

    def finish(self, out):
        plane, planes = self.plane, self.planes

        @pl.when(plane == 0)
        def _():
            self.down(plane).wait_recv()
            out[...] = self.stack[plane] + self.came[planes]

        @pl.when(plane == planes - 1)
        def _():
            self.up(plane).wait_recv()
            out[...] = self.stack[plane] + self.came[plane]

        @pl.when((plane > 0) & (plane < planes - 1))
        def _():
            self.up(plane).wait_recv()
            self.down(plane).wait_recv()
            total = self.stack[plane].astype(F32) + self.came[plane].astype(F32)
            out[...] = (total + self.came[planes].astype(F32)).astype(BF16)

        for j in range(planes):
            ups, downs = plane < j, plane > j
            if self.paced and j > 1:
                ups = ups & (plane > 0)
            if self.paced and j < planes - 2:
                downs = downs & (plane < planes - 1)
            pl.when(ups)(lambda j=j: self.up(j).wait_send())
            pl.when(downs)(lambda j=j: self.down(j).wait_send())

    def fill_rows(self, left, left_came, right, right_came):
        shard = self.stack.shape[1]

        def body(j, carry):
            at = pl.ds(pl.multiple_of(j * shard, shard), shard)
            self.stack[j] = (
                dot(left[:, at], right[...], TN) + dot(left_came[:, at], right_came[...], TN)
            ).astype(BF16)
            return carry

        lax.fori_loop(0, self.planes, body, 0)

    def fill_columns(self, left, left_came, right, right_came):
        shard = self.stack.shape[2]
        tile = 256

        def body(t, carry):
            at = pl.ds(pl.multiple_of(t * tile, tile), tile)
            term = dot(left[:, at], right[...], TN) + dot(left_came[:, at], right_came[...], TN)
            for j in range(self.planes):
                self.stack[j, at, :] = term[:, j * shard : (j + 1) * shard].astype(BF16)
            return carry

        lax.fori_loop(0, left.shape[1] // tile, body, 0)


class TensorSum:
    def __init__(self, scratch, mine, core, core_peer, y_peer):
        self.away, self.core_came, self.both, self.y_came = scratch[:4]
        self.sems = scratch[4:]
        self.mine = mine
        self.core, self.core_peer, self.y_peer = core, core_peer, y_peer
        self.chunks, self.half, self.width = self.away.shape

    @staticmethod
    def scratch(chunks, half, width):
        return [pltpu.VMEM((chunks, half, width), BF16)] * 4 + [
            pltpu.SemaphoreType.DMA((chunks,))
        ] * 4

    def over_core(self, i):
        s = self.sems
        return remote(self.away.at[i], self.core_came.at[i], s[0].at[i], s[1].at[i], self.core_peer)

    def over_y(self, i):
        s = self.sems
        return remote(self.both.at[i], self.y_came.at[i], s[2].at[i], s[3].at[i], self.y_peer)

    def add(self, i, value):
        self.mine[i % 2] = value
        self.away[i] = self.mine[i % 2, rows_of(1 - self.core, self.half), :].astype(BF16)
        self.over_core(i).start()
        if i > 0:
            self.pass_on(i - 1)
        if i == self.chunks - 1:
            self.pass_on(i)

    def pass_on(self, i):
        self.over_core(i).wait_recv()
        mine = self.mine[i % 2, rows_of(self.core, self.half), :]
        self.both[i] = (mine + self.core_came[i].astype(F32)).astype(BF16)
        self.over_y(i).start()

    def total(self, i):
        self.over_y(i).wait_recv()
        return self.both[i].astype(F32) + self.y_came[i].astype(F32)

    def finish(self):
        for i in range(self.chunks):
            self.over_core(i).wait_send()
            self.over_y(i).wait_send()


def roll_half(value):
    return pltpu.roll(value, value.shape[-1] // 2, 1)


def visible(shape, key0, row0, prefix):
    key_pos = key0 + lax.broadcasted_iota(jnp.int32, shape, 1)
    row_pos = row0 + lax.broadcasted_iota(jnp.int32, shape, 0)
    return (key_pos <= row_pos) | (key_pos < prefix)


def attn_fwd_kernel(*refs, group, kv_heads, repeat, width, tile, coef):
    refs = list(refs)

    def take(count):
        out = refs[:count]
        del refs[:count]
        return out

    prefix_ref, gain_ref, q_gain, k_gain = take(4)
    arrays = take(6)
    o_ref, lse_ref, all_out = take(3)
    outs = take(4)
    buffers = take(6)
    inputs = Staged(arrays, buffers, *take(1))
    x_ref, w_k, w_v, cos_ref, sin_ref, w_q = buffers
    out_buffers = take(4)
    h_ref, q_ref, q_raw, k_raw = out_buffers
    outputs = Staged(outs, out_buffers, *take(1), out=True)
    kv_ref, all_ref, all_sems, acc, send_x, recv_x, send_z, recv_z, send_down = take(9)
    rows = q_ref.shape[0]
    kv_width = kv_heads * width
    planes = group // 2
    device = lax.axis_index("dp")
    member = device % group
    plane = member // 2
    x_at = member % 2
    x_other = device + 1 - 2 * x_at
    inner = plane < planes - 1
    prefix = prefix_ref[0]
    inputs.start()
    greet([({"dp": x_other}, True), ({"dp": device + 2}, inner), ({"dp": device - 2}, plane > 0)])

    def store(slot):
        return pltpu.make_async_copy(all_ref.at[slot], all_out.at[slot], all_sems.at[slot])

    def source(slot):
        return kv_ref if slot == 0 else all_ref.at[2 * slot]

    def to_x(slot):
        return pltpu.make_async_remote_copy(
            src_ref=source(slot),
            dst_ref=all_ref.at[2 * slot + 1],
            send_sem=send_x.at[slot],
            recv_sem=recv_x.at[slot],
            device_id={"dp": x_other},
            device_id_type=pl.DeviceIdType.MESH,
        )

    def to_z(slot):
        return pltpu.make_async_remote_copy(
            src_ref=source(slot - 1),
            dst_ref=all_ref.at[2 * slot],
            send_sem=send_z.at[slot],
            recv_sem=recv_z.at[slot],
            device_id={"dp": device + 2},
            device_id_type=pl.DeviceIdType.MESH,
        )

    def to_first():
        return pltpu.make_async_remote_copy(
            src_ref=kv_ref,
            dst_ref=all_ref.at[2],
            send_sem=send_down,
            recv_sem=recv_z.at[1],
            device_id={"dp": device - 2},
            device_id_type=pl.DeviceIdType.MESH,
        )

    inputs.wait(x_ref, w_k, w_v, cos_ref, sin_ref)
    x = x_ref[...].astype(F32)
    r = lax.rsqrt(jnp.mean(x * x, axis=1, keepdims=True) + EPS)
    h_ref[...] = (x * r * gain_ref[...]).astype(BF16)
    cos, sin = cos_ref[...], sin_ref[...]

    def rotate(u, gain):
        u = u * lax.rsqrt(jnp.mean(u * u, axis=1, keepdims=True) + EPS) * gain[...]
        return (u * cos + roll_half(u) * sin).astype(BF16)

    keys = dot(h_ref[...], w_k[...])
    k_raw[...] = keys
    for at in range(0, kv_width, width):
        kv_ref[:, at : at + width] = rotate(keys[:, at : at + width], k_gain)
    kv_ref[:, kv_width:] = dot(h_ref[...], w_v[...]).astype(BF16)
    ones = jnp.ones((rows, width), BF16)
    row0 = member * rows

    def work(block, other, masked, start=False):
        key0 = other * rows

        def head_pair(h, carry):
            k = block[:, pl.ds(pl.multiple_of(h * width, width), width)]
            v = block[:, pl.ds(pl.multiple_of(kv_width + h * width, width), width)]
            v = jnp.concatenate([v, ones], axis=1)
            for g in range(repeat):
                head = h * repeat + g
                for at in range(0, rows, tile):
                    q = q_ref[at : at + tile, pl.ds(pl.multiple_of(head * width, width), width)]
                    p = jnp.exp2(dot(q, k, NT) * coef)
                    if masked:
                        p = jnp.where(visible(p.shape, key0, row0 + at, prefix), p, 0.0)
                    term = dot(p.astype(BF16), v)
                    if start:
                        acc[head, at : at + tile, :] = term
                    else:
                        acc[head, at : at + tile, :] += term
            return carry

        lax.fori_loop(0, kv_heads, head_pair, 0)

    to_x(0).start()
    if planes > 1:

        @pl.when(inner)
        def _():
            to_z(1).start()

        @pl.when(plane == 1)
        def _():
            to_first().start()

    inputs.wait(w_q)
    queries = dot(h_ref[...], w_q[...])
    q_raw[...] = queries
    for at in range(0, queries.shape[1], width):
        q_ref[:, at : at + width] = rotate(queries[:, at : at + width], q_gain)
    outputs.start()
    all_ref[0] = kv_ref[...]
    store(0).start()
    work(kv_ref, member, True, True)
    to_x(0).wait_recv()
    store(1).start()
    work(all_ref.at[1], member + 1 - 2 * x_at, True)
    for slot in range(1, planes):

        def step(slot=slot):
            to_z(slot).wait_recv()
            if slot < planes - 1:

                @pl.when(inner & (plane >= slot))
                def _():
                    to_z(slot + 1).start()

            to_x(slot).start()
            store(2 * slot).start()
            there = 2 * (plane - slot)
            if slot == 1:

                @pl.when(plane == 0)
                def _():
                    work(all_ref.at[2 * slot], 2 + x_at, True)

                @pl.when(plane > 0)
                def _():
                    work(all_ref.at[2 * slot], there + x_at, False)
            else:
                work(all_ref.at[2 * slot], there + x_at, False)
            to_x(slot).wait_recv()
            store(2 * slot + 1).start()
            if slot == 1:

                @pl.when(plane == 0)
                def _():
                    work(all_ref.at[2 * slot + 1], 3 - x_at, True)

                @pl.when(plane > 0)
                def _():
                    work(all_ref.at[2 * slot + 1], there + 1 - x_at, False)
            else:
                work(all_ref.at[2 * slot + 1], there + 1 - x_at, False)

        if slot == 1:
            step()
        else:
            pl.when(plane >= slot)(step)

    for head in range(kv_heads * repeat):
        total = acc[head, :, width:]
        o_ref[:, head * width : (head + 1) * width] = (acc[head, :, :width] / total).astype(BF16)
        lse_ref[:, head * width : (head + 1) * width] = jnp.log2(total) * (1.0 / coef)

    outputs.wait()
    to_x(0).wait_send()
    for slot in range(planes):

        @pl.when((plane >= slot) | (slot <= 1))
        def _(slot=slot):
            store(2 * slot).wait()
            store(2 * slot + 1).wait()

    for slot in range(1, planes):

        @pl.when(inner & (plane >= slot - 1))
        def _(slot=slot):
            to_z(slot).wait_send()

        @pl.when((plane >= slot) | (slot == 1))
        def _(slot=slot):
            to_x(slot).wait_send()

    if planes > 1:

        @pl.when(plane == 1)
        def _():
            to_first().wait_send()


def attn_fwd(prefix, x, gain, w_query, key_weight, value_weight, q_gain, k_gain, cos, sin, group, dims):
    kv_heads, repeat, width = dims
    rows = x.shape[0]
    heads = kv_heads * repeat
    columns = heads * width
    planes = group // 2
    dma = pltpu.SemaphoreType.DMA
    block = (rows, 2 * kv_heads * width)
    staged = [x, key_weight, value_weight, cos, sin, w_query]
    early = [
        jax.ShapeDtypeStruct(x.shape, BF16),
        jax.ShapeDtypeStruct((rows, columns), BF16),
        jax.ShapeDtypeStruct((rows, columns), F32),
        jax.ShapeDtypeStruct((rows, kv_heads * width), F32),
    ]
    return pl.pallas_call(
        functools.partial(
            attn_fwd_kernel,
            group=group,
            kv_heads=kv_heads,
            repeat=repeat,
            width=width,
            tile=min(rows, 256),
            coef=math.log2(math.e) / math.sqrt(width),
        ),
        out_shape=[
            jax.ShapeDtypeStruct((rows, columns), BF16),
            jax.ShapeDtypeStruct((rows, columns), F32),
            jax.ShapeDtypeStruct((group,) + block, BF16),
        ]
        + early,
        in_specs=[smem()] + vmem(3) + [ANYWHERE] * 6,
        out_specs=vmem(2) + [ANYWHERE] * 5,
        scratch_shapes=Staged.scratch(staged)
        + Staged.scratch(early)
        + [pltpu.VMEM(block, BF16), pltpu.VMEM((group,) + block, BF16), dma((group,))]
        + [pltpu.VMEM((heads, rows, 2 * width), F32)]
        + [dma((planes,))] * 4
        + [dma],
        compiler_params=pltpu.CompilerParams(
            vmem_limit_bytes=VMEM_LIMIT, collective_id=0, has_side_effects=True
        ),
        cost_estimate=COST,
        name="attn_fwd",
    )(prefix, gain, q_gain, k_gain, *staged)


def split_three(value):
    high = value.astype(BF16)
    left = value - high.astype(F32)
    mid = left.astype(BF16)
    return high.astype(F32), mid.astype(F32), (left - mid.astype(F32)).astype(BF16).astype(F32)


def back_kernel(
    *refs, group, planes, all_planes, shard, kv_heads, repeat, width, coef, scale, sums
):
    refs = list(refs)

    def take(count):
        out = refs[:count]
        del refs[:count]
        return out

    device = lax.axis_index("dp")
    member = device % group
    plane = member // 2
    last = planes - 1
    prefix_ref, up_ref, w_down_in, middle_in = take(4)
    if sums:
        hid_arrays = take(1)
    count = 12 if sums else 5
    arrays = take(count)
    dq_ref, grad_ref, a_ref, a_came_ref, up_came_ref, block_ref = take(6)
    if sums:
        w_down_ref, w_gate_ref, w_out_ref = take(3)
    if sums:
        hid_buffers = take(1)
        hid_sems = take(1)[0]
    buffers = take(count)
    inputs = Staged(arrays, buffers, *take(1))
    a_all_ref, qx_ref, dox_ref, kv_ref, hid_ref = buffers[:5]
    if sums:
        hid_came_ref = hid_buffers[0]
        og_ref, og_came_ref, gate_ref, h_ref, h_came_ref, heads_ref, heads_came_ref = buffers[5:]
    down_buf, down_sems, mine_ref, middle_buf, middle_sems = take(5)
    block_sems = take(3)
    total_scratch = take(8)
    own_ref, far_ref, xr_ref, zr_ref, first_ref = take(5)
    send_x, recv_x, send_z, recv_z, send_first, recv_first = take(6)
    swap_sems = take(2)
    a_scratch = take(6)
    rows = qx_ref.shape[1]
    kv_width = kv_heads * width
    if sums:
        gate_came_ref, send_gate, recv_gate = take(3)
        left = w_down_ref.shape[0]
        rest = pl.ds(hid_arrays[0].shape[1] - left, left)
        hid_inputs = Staged([h.at[:, rest] for h in hid_arrays], hid_buffers, hid_sems)
        down_sum, out_sum = (LineSum(take(6), device, plane, planes) for _ in range(2))
        piece = gate_came_ref.shape[2]
        pieces = gate_ref.shape[1] // piece
        gate_sums = [LineSum(take(6), device, plane, planes) for _ in range(pieces)]
    x_at = member % 2
    x_other = device + 1 - 2 * x_at
    inner = plane < last
    prefix = prefix_ref[0]

    core, core_peer, y_peer = tensor_peers()
    x_peer = {"dp": x_other}
    total = TensorSum(total_scratch, mine_ref, core, core_peer, y_peer)
    half = total.half
    parts, narrow = total.chunks, total.width

    def load(i):
        at = pl.ds(i * narrow, narrow)
        return pltpu.make_async_copy(w_down_in.at[:, at], down_buf.at[i % 2], down_sems.at[i % 2])

    def middle_load(i):
        at = pl.ds(i * narrow, narrow)
        return pltpu.make_async_copy(middle_in.at[:, at], middle_buf.at[i % 2], middle_sems.at[i % 2])

    def block_at(i):
        return block_ref.at[rows_of(core, half), pl.ds(i * narrow, narrow)]

    def block_store(i):
        return pltpu.make_async_copy(total.both.at[i], block_at(i), block_sems[0].at[i])

    def block_give(i):
        return remote(total.both.at[i], block_at(i), block_sems[1].at[i], block_sems[2].at[i], core_peer)

    def block_add(i):
        load(i).wait()
        total.add(i, dot(hid_ref[...], down_buf[i % 2]))
        if i + 2 < parts:
            load(i + 2).start()

    def block_finish(i):
        middle_load(i).wait()
        value = middle_buf[i % 2] + total.total(i)
        total.over_y(i).wait_send()
        total.both[i] = value.astype(BF16)
        if i + 2 < parts:
            middle_load(i + 2).start()
        block_store(i).start()
        block_give(i).start()

    inputs.start(a_all_ref)
    if sums:
        hid_inputs.start()
        inputs.start(hid_ref, *buffers[5:7])
    inputs.start(*buffers[1:4])
    if sums:
        inputs.start(*buffers[7:])
    else:
        inputs.start(hid_ref)
    for i in range(2):
        load(i).start()
        middle_load(i).start()
    greet(
        [
            (x_peer, True),
            (core_peer, True),
            (y_peer, True),
            ({"dp": device + 2}, inner),
            ({"dp": device - 2}, plane > 0),
        ]
    )

    def copy(src, dst, send, recv, there):
        return remote(src, dst, send, recv, {"dp": there})

    place = (x_at, core, x_peer, core_peer, all_planes, shard)
    d_attn = Columns(a_all_ref, a_ref, a_came_ref, a_scratch, *place)
    up_swap = copy(up_ref, up_came_ref, swap_sems[0], swap_sems[1], x_other)

    def gate_swap(k):
        part = gate_ref.at[:, pl.ds(k * piece, piece)]
        return copy(part, gate_came_ref.at[k], send_gate.at[k], recv_gate.at[k], x_other)

    def gate_start(k):
        gate_swap(k).wait_recv()
        part = gate_ref.at[:, pl.ds(k * piece, piece)]
        gate_sums[k].fill_rows(h_ref, h_came_ref, part, gate_came_ref.at[k])
        gate_sums[k].start()

    lane = lax.broadcasted_iota(jnp.int32, (rows, width), 1)
    minus = jnp.where(lane < 3, -1.0, 0.0).astype(BF16)
    row0 = member * rows

    def work(block, other, masked, out):
        key0 = other * rows

        def head_group(h, carry):
            k_at = pl.ds(pl.multiple_of(h * width, width), width)
            v_at = pl.ds(pl.multiple_of(kv_width + h * width, width), width)
            k = kv_ref[block, :, k_at]
            v = kv_ref[block, :, v_at]
            kx = jnp.concatenate([k, minus], axis=1)
            vx = jnp.concatenate([v, minus], axis=1)
            dk = jnp.zeros((rows, width), F32)
            dv = jnp.zeros((rows, width), F32)
            for g in range(repeat):
                head = h * repeat + g
                qx = qx_ref[head]
                dox = dox_ref[head]
                p = jnp.exp2(dot(qx, kx, NT) * coef)
                if masked:
                    p = jnp.where(visible(p.shape, key0, row0, prefix), p, 0.0)
                ds = (p * dot(dox, vx, NT)).astype(BF16)
                dv += dot(p.astype(BF16), dox[:, :width], TN)
                dk += dot(ds, qx[:, :width], TN)
                dq_ref[:, pl.ds(pl.multiple_of(head * width, width), width)] += dot(ds, k)
            out[:, k_at] = (dk * scale).astype(BF16)
            out[:, v_at] = dv.astype(BF16)
            return carry

        lax.fori_loop(0, kv_heads, head_group, 0)

    def far_swap(slot):
        return copy(far_ref.at[slot], xr_ref.at[slot], send_x.at[slot], recv_x.at[slot], x_other)

    def to_plane(slot):
        return copy(own_ref.at[slot], zr_ref.at[slot], send_z.at[slot], recv_z.at[slot], device - 2)

    def from_first():
        return copy(own_ref.at[1], first_ref, send_first, recv_first, device + 2)

    def attend(slot):
        there = 2 * (plane - slot)
        far, own = there + 1 - x_at, there + x_at

        def both(far, own, masked):
            work(2 * slot + 1, far, masked, far_ref.at[slot])
            far_swap(slot).start()
            work(2 * slot, own, masked, own_ref.at[slot])

        if slot == 0:
            both(far, own, True)
        elif slot == 1:
            pl.when(plane == 0)(lambda: both(3 - x_at, 2 + x_at, True))
            pl.when(plane > 0)(lambda: both(far, own, False))
        else:
            pl.when(plane >= slot)(lambda: both(far, own, False))

    def pass_back(slot):
        def go():
            far_swap(slot).wait_recv()
            own_ref[slot] += xr_ref[slot]
            if slot < last:

                @pl.when(inner & (plane >= slot))
                def _():
                    to_plane(slot + 1).wait_recv()
                    own_ref[slot] += zr_ref[slot + 1]

            if slot == 1:
                pl.when(plane == 0)(lambda: from_first().start())
                pl.when(plane > 0)(lambda: to_plane(slot).start())
            else:
                to_plane(slot).start()

        if slot == 1:
            go()
        else:
            pl.when(plane >= slot)(go)

    dq_ref[...] = jnp.zeros_like(dq_ref)
    inputs.wait(a_all_ref)
    d_attn.start()
    inputs.wait(hid_ref)
    if sums:
        hid_inputs.wait()
        inputs.wait(og_ref, og_came_ref)
        down_sum.fill_columns(hid_ref.at[:, rest], hid_came_ref, og_ref, og_came_ref)
        down_sum.start()
    inputs.wait(*buffers[1:4])
    attend(last)
    d_attn.forward()
    if sums:
        inputs.wait(*buffers[7:])
        gate_swap(0).start()
    d_attn.store()
    pending = list(range(last, 0, -1))
    steps = range(1, last)
    adds = list(range(parts))
    share = -(-parts // last)
    for slot in range(last - 1, -1, -1):
        attend(slot)
        if slot == last - 1:
            if sums:
                d_attn.over_core().wait_recv()
                out_sum.fill_columns(heads_ref, heads_came_ref, a_ref, a_came_ref)
                out_sum.start()
                down_sum.advance(1)
                gate_start(0)
                gate_swap(1).start()
            pass_back(pending.pop(0))
        if slot == last - 2:
            if sums:
                for step in steps[1:]:
                    down_sum.advance(step)
                out_sum.advance(1)
                gate_start(1)
                gate_swap(2).start()
                gate_sums[0].advance(1)
            pass_back(pending.pop(0))
        for i in adds[:share]:
            block_add(i)
        del adds[:share]
    for i in adds:
        block_add(i)
    if sums:
        for step in steps[1:]:
            out_sum.advance(step)
            gate_sums[0].advance(step)
    while pending:
        pass_back(pending.pop(0))
    if sums:
        gate_start(2)
    up_swap.start()
    if sums:
        gate_sums[1].advance(1)
    for i in range(parts // 2):
        block_finish(i)
    if sums:
        for step in steps[1:]:
            gate_sums[1].advance(step)
        gate_sums[2].advance(1)
    for i in range(parts // 2, parts):
        block_finish(i)
    if sums:
        for step in steps[1:]:
            gate_sums[2].advance(step)
    dq_ref[...] = dq_ref[...] * scale

    far_swap(0).wait_recv()
    grad_ref[...] = own_ref[0].astype(F32) + xr_ref[0].astype(F32)
    if last > 0:

        @pl.when(inner)
        def _():
            to_plane(1).wait_recv()
            grad_ref[...] += zr_ref[1].astype(F32)

        @pl.when(plane == 1)
        def _():
            from_first().wait_recv()
            grad_ref[...] += first_ref[...].astype(F32)

    if sums:
        down_sum.finish(w_down_ref)
        out_sum.finish(w_out_ref)
        for k in range(pieces):
            gate_sums[k].finish(w_gate_ref.at[:, pl.ds(k * piece, piece)])
            gate_swap(k).wait_send()
    else:
        d_attn.over_core().wait_recv()
    up_swap.wait_recv()
    up_swap.wait_send()
    for i in range(parts):
        total.over_core(i).wait_send()
        block_store(i).wait()
        block_give(i).wait_recv()
        block_give(i).wait_send()
    d_attn.over_x().wait_send()
    d_attn.over_core().wait_send()
    for slot in range(planes):
        if slot <= 1:
            far_swap(slot).wait_send()
        else:
            pl.when(plane >= slot)(lambda slot=slot: far_swap(slot).wait_send())
        if slot >= 1:
            pl.when(plane >= slot)(lambda slot=slot: to_plane(slot).wait_send())
    if last > 0:
        pl.when(plane == 0)(lambda: from_first().wait_send())


def back(prefix, qx, dox, kv_all, shared, grads, group, all_planes, shard, pieces, dims):
    kv_heads, repeat, width = dims
    rows = qx.shape[1]
    columns = kv_heads * repeat * width
    planes = group // 2
    block = kv_all.shape[1:]
    dma = pltpu.SemaphoreType.DMA
    d_attn, d_up, hidden, w_down, middle = shared
    half, model = middle.shape
    parts = 8
    narrow = model // parts
    units = d_up.shape[1]
    cut_shape = jax.ShapeDtypeStruct((rows, all_planes * shard), BF16)
    out_shape = [jax.ShapeDtypeStruct((rows, columns), F32), jax.ShapeDtypeStruct(block, F32)]
    out_shape += [cut_shape] * 2 + [jax.ShapeDtypeStruct(d_up.shape, BF16)]
    out_shape.append(jax.ShapeDtypeStruct((rows, model), BF16))
    scratch = [pltpu.VMEM((planes,) + block, BF16)] * 4 + [pltpu.VMEM(block, BF16)]
    scratch += [dma((planes,))] * 4 + [dma, dma] + [dma] * 2
    scratch += Columns.scratch(rows // 2, all_planes * shard)
    staged = [d_attn, qx, dox, kv_all, hidden]
    args = [prefix, d_up, w_down, middle]
    first = []
    if grads is not None:
        args += grads[:1]
        staged += grads[1:]
        first = [pltpu.VMEM((rows, units // pieces), BF16), dma((1,))]
    args += staged
    product = [pltpu.VMEM((2, units, narrow), BF16), dma((2,)), pltpu.VMEM((2, rows, narrow), F32)]
    product += [pltpu.VMEM((2, half, narrow), F32), dma((2,))] + [dma((parts,))] * 3
    product += TensorSum.scratch(parts, half, narrow)
    scratch = first + Staged.scratch(staged) + product + scratch
    if grads is not None:
        piece = units // pieces
        shapes = (piece, shard), (shard, units), (columns, shard)
        out_shape += [jax.ShapeDtypeStruct(s, BF16) for s in shapes]
        scratch += [pltpu.VMEM((pieces, rows, piece), BF16)] + [dma((pieces,))] * 2
        for shape in [(piece, shard), (columns, shard)] + [(shard, piece)] * pieces:
            scratch += LineSum.scratch(planes, shape)
    return pl.pallas_call(
        functools.partial(
            back_kernel,
            group=group,
            planes=planes,
            all_planes=all_planes,
            shard=shard,
            kv_heads=kv_heads,
            repeat=repeat,
            width=width,
            coef=math.log2(math.e) / math.sqrt(width),
            scale=1.0 / math.sqrt(width),
            sums=grads is not None,
        ),
        out_shape=out_shape,
        in_specs=[smem()] + [ANYWHERE] * (len(args) - 1),
        out_specs=vmem(4) + [ANYWHERE] * 2 + vmem(len(out_shape) - 6),
        scratch_shapes=scratch,
        compiler_params=pltpu.CompilerParams(
            vmem_limit_bytes=BACK_VMEM_LIMIT, collective_id=1, has_side_effects=True
        ),
        cost_estimate=COST,
        name="back",
    )(*args)


def smem():
    return pl.BlockSpec(memory_space=pltpu.SMEM)


def out_kernel(*refs, planes, shard, blocks):
    refs = list(refs)

    def take(count):
        out = refs[:count]
        del refs[:count]
        return out

    arrays = take(4)
    gain_ref, w_down_ref = take(2)
    middle_ref, h_ref, d_hidden_out, og_keep, og_came, heads_came = take(6)
    buffers = take(4)
    heads_ref, w_ref, og_ref, x_ref = buffers
    inputs = Staged(arrays, buffers, *take(1))
    d_hidden_ref, d_hidden_sem = take(2)
    down_buf, down_sems, mine_ref, h_send, h_recv, heads_send, heads_recv = take(7)
    scratch = refs
    device = lax.axis_index("dp")
    core, core_peer, y_peer = tensor_peers()
    x_at = device % 2
    x_peer = {"dp": device + 1 - 2 * x_at}
    half = middle_ref.shape[0]
    total = TensorSum(scratch[:8], mine_ref, core, core_peer, y_peer)
    chunks, width = total.chunks, total.width
    place = (x_at, core, x_peer, core_peer, planes, shard)
    og = Columns(og_ref, og_keep, og_came, scratch[8:14], *place)
    tiles = down_sems.shape[0]
    tile = down_buf.shape[0] // tiles

    def load(t):
        at = pl.ds(t * tile, tile)
        return pltpu.make_async_copy(w_down_ref.at[at, :], down_buf.at[at, :], down_sems.at[t])

    inputs.start()
    for t in range(tiles):
        load(t).start()
    greet([(x_peer, True), (core_peer, True), (y_peer, True)])
    heads_swap = remote(heads_ref, heads_came, heads_send, heads_recv, x_peer)
    inputs.wait(heads_ref, w_ref)
    heads_swap.start()
    for i in range(chunks):
        total.add(i, dot(heads_ref[...], w_ref[:, i * width : (i + 1) * width]))
    inputs.wait(og_ref)
    og.start()
    og.store()
    for t in range(tiles):
        at = slice(t * tile, (t + 1) * tile)
        load(t).wait()
        d_hidden_ref[:, at] = dot(og_ref[...], down_buf[at, :], NT)
    d_hidden_copy = pltpu.make_async_copy(d_hidden_ref, d_hidden_out, d_hidden_sem)
    d_hidden_copy.start()
    mine = rows_of(core, half)
    inputs.wait(x_ref)
    for i in range(chunks):
        at = slice(i * width, (i + 1) * width)
        middle_ref[:, at] = x_ref[mine, at].astype(F32) + total.total(i)
    step = half // blocks

    def to_core(b):
        rows = h_ref.at[pl.ds(pl.multiple_of(core * half + b * step, step), step), :]
        return remote(rows, rows, h_send.at[b], h_recv.at[b], core_peer)

    for b in range(blocks):
        v = middle_ref[b * step : (b + 1) * step, :]
        r = lax.rsqrt(jnp.mean(v * v, axis=1, keepdims=True) + EPS)
        at = pl.ds(pl.multiple_of(core * half + b * step, step), step)
        h_ref[at, :] = (v * r * gain_ref[...]).astype(BF16)
        to_core(b).start()
    og.forward()
    og.finish()
    d_hidden_copy.wait()
    heads_swap.wait_recv()
    heads_swap.wait_send()
    for b in range(blocks):
        to_core(b).wait_recv()
        to_core(b).wait_send()
    total.finish()


def attention_out(heads, w_out, x, gain, out_grad, w_down, planes, shard):
    rows, model = x.shape
    half = rows // 2
    units = w_down.shape[0]
    chunks, blocks = 4, 4
    tiles = units // math.gcd(units, 256)
    dma = pltpu.SemaphoreType.DMA
    cut_shape = jax.ShapeDtypeStruct((rows, planes * shard), BF16)
    return pl.pallas_call(
        functools.partial(out_kernel, planes=planes, shard=shard, blocks=blocks),
        out_shape=[
            jax.ShapeDtypeStruct((half, model), F32),
            jax.ShapeDtypeStruct((rows, model), BF16),
            jax.ShapeDtypeStruct((rows, units), F32),
        ]
        + [cut_shape] * 2
        + [jax.ShapeDtypeStruct(heads.shape, BF16)],
        in_specs=[ANYWHERE] * 4 + vmem(1) + [ANYWHERE],
        out_specs=vmem(2) + [ANYWHERE] + vmem(3),
        scratch_shapes=Staged.scratch([heads, w_out, out_grad, x])
        + [pltpu.VMEM((rows, units), F32), dma]
        + [pltpu.VMEM((units, model), BF16), dma((tiles,))]
        + [pltpu.VMEM((2, rows, model // chunks), F32), dma((blocks,)), dma((blocks,)), dma, dma]
        + TensorSum.scratch(chunks, half, model // chunks)
        + Columns.scratch(half, planes * shard),
        compiler_params=pltpu.CompilerParams(
            vmem_limit_bytes=VMEM_LIMIT, collective_id=4, has_side_effects=True
        ),
        cost_estimate=COST,
        name="attention_out",
    )(heads, w_out, out_grad, x, gain, w_down)


def middle_kernel(*refs, planes, shard, heads, width, pieces, blocks, sums):
    refs = list(refs)

    def take(count):
        out = refs[:count]
        del refs[:count]
        return out

    w_gate_ref, w_up_ref, gain_ref = take(3)
    count = 10 if sums else 8
    arrays = take(count)
    outs = take(3)
    hid_came_ref, a_ref, gain_out_ref, qx_ref, dox_ref, h_keep, h_came = take(7)
    if sums:
        down_outs = take(pieces - 1)
    buffers = take(count)
    inputs = Staged(arrays, buffers, *take(1))
    h_ref, d_ref, middle_ref, og_ref, w_out_ref, q_ref, o_ref, lse_ref = buffers[:8]
    if sums:
        og_keep, og_came = buffers[8:]
    out_buffers = take(3)
    hid_ref, gate_ref, up_ref = out_buffers
    outputs = Staged(outs, out_buffers, *take(1), out=True)
    gate_buf, up_buf, load_sems, c_ref, mine_ref = take(5)
    hid_send, hid_recv, a_send, a_recv = take(4)
    sum_scratch, h_scratch = take(8), take(6)
    device = lax.axis_index("dp")
    core, core_peer, y_peer = tensor_peers()
    plane = device // 2
    x_at = device % 2
    x_peer = {"dp": device + 1 - 2 * x_at}
    meets = [(x_peer, True), (core_peer, True), (y_peer, True)]
    h_two = Columns(h_ref, h_keep, h_came, h_scratch, x_at, core, x_peer, core_peer, planes, shard)
    half = middle_ref.shape[0]
    total = TensorSum(sum_scratch, mine_ref, core, core_peer, y_peer)
    chunks, columns = total.chunks, total.width
    units = hid_ref.shape[1]
    piece = units // pieces
    tile = 256
    tiles = units // tile
    if sums:
        downs = [LineSum(take(6), device, plane, planes) for _ in range(pieces - 1)]
        meets += [({"dp": device + 2}, plane < planes - 1), ({"dp": device - 2}, plane > 0)]

    def loads(t):
        at = pl.ds(t * tile, tile)
        return (
            pltpu.make_async_copy(w_gate_ref.at[:, at], gate_buf.at[:, at], load_sems.at[2 * t]),
            pltpu.make_async_copy(w_up_ref.at[:, at], up_buf.at[:, at], load_sems.at[2 * t + 1]),
        )

    inputs.start(h_ref)
    for t in range(tiles):
        for load in loads(t):
            load.start()
        if t == 0:
            inputs.start(d_ref)
    inputs.start(*buffers[2:])
    greet(meets)
    inputs.wait(h_ref)

    def swap(k):
        at = pl.ds(k * piece, piece)
        return remote(hid_ref.at[:, at], hid_came_ref.at[:, at], hid_send.at[k], hid_recv.at[k], x_peer)

    for t in range(tiles):
        for load in loads(t):
            load.wait()
        if t == 0:
            inputs.wait(d_ref)
        at = slice(t * tile, (t + 1) * tile)
        gate = dot(h_ref[...], gate_buf[:, at])
        up = dot(h_ref[...], up_buf[:, at])
        sig = 1.0 / (1.0 + jnp.exp(-gate))
        silu = gate * sig
        d = d_ref[:, at]
        hid_ref[:, at] = (silu * up).astype(BF16)
        up_ref[:, at] = (d * silu).astype(BF16)
        gate_ref[:, at] = (d * up * (sig * (1.0 + gate * (1.0 - sig)))).astype(BF16)
        if (t + 1) * tile % piece == 0:
            swap((t + 1) * tile // piece - 1).start()

    outputs.start()
    inputs.wait(*buffers[2:])

    def down_start(k):
        if sums:
            at = pl.ds(k * piece, piece)
            swap(k).wait_recv()
            downs[k].fill_columns(hid_ref.at[:, at], hid_came_ref.at[:, at], og_keep, og_came)
            downs[k].start()

    def down_advance(k, step):
        if sums and step <= planes - 2:
            downs[k].advance(step)

    for i in range(chunks):
        at = slice(i * columns, (i + 1) * columns)
        total.add(i, dot(gate_ref[...], gate_buf[at, :], NT) + dot(up_ref[...], up_buf[at, :], NT))
        if i == chunks - 2:
            down_start(0)
    for i in range(chunks):
        if i == 1:
            down_start(1)
            h_two.start()
        if i == 2:
            down_advance(0, 1)
        c_ref[:, i * columns : (i + 1) * columns] = total.total(i)
    down_advance(0, 2)

    step = half // blocks

    def to_core(b):
        rows = a_ref.at[pl.ds(pl.multiple_of(core * half + b * step, step), step), :]
        return remote(rows, rows, a_send.at[b], a_recv.at[b], core_peer)

    gain_out_ref[...] = jnp.zeros_like(gain_out_ref)
    for b in range(blocks):
        at = slice(b * step, (b + 1) * step)
        whole_at = pl.ds(pl.multiple_of(core * half + b * step, step), step)
        c = c_ref[at, :]
        v = middle_ref[at, :]
        r = lax.rsqrt(jnp.mean(v * v, axis=1, keepdims=True) + EPS)
        n = v * r
        gain_out_ref[...] += jnp.sum(c * n, axis=0, keepdims=True)
        gc = c * gain_ref[...]
        d = r * (gc - n * jnp.mean(n * gc, axis=1, keepdims=True)) + og_ref[whole_at, :].astype(F32)
        a_ref[whole_at, :] = d.astype(BF16)
        to_core(b).start()

    lane = lax.broadcasted_iota(jnp.int32, (half, width), 1)

    def extra(value):
        a, b, c = split_three(value)
        return jnp.where(lane == 0, a, jnp.where(lane == 1, b, jnp.where(lane == 2, c, 0.0))).astype(BF16)

    def prepare(which):
        at_rows = rows_of(which, half)
        d_heads = dot(a_ref[at_rows, :], w_out_ref[...], NT)
        for head in range(heads):
            at = slice(head * width, (head + 1) * width)
            qx_ref[head, at_rows, :width] = q_ref[at_rows, at]
            qx_ref[head, at_rows, width:] = extra(lse_ref[at_rows, at])
            d = d_heads[:, at].astype(BF16)
            delta = jnp.sum(d.astype(F32) * o_ref[at_rows, at].astype(F32), axis=1, keepdims=True)
            dox_ref[head, at_rows, :width] = d
            dox_ref[head, at_rows, width:] = extra(jnp.broadcast_to(delta, (half, width)))

    down_advance(1, 1)
    h_two.store()
    prepare(core)
    h_two.forward()
    for b in range(blocks):
        to_core(b).wait_recv()
    prepare(1 - core)
    down_advance(1, 2)
    for b in range(blocks):
        to_core(b).wait_send()
    total.finish()
    h_two.finish()
    outputs.wait()
    for k in range(pieces):
        if k == pieces - 1 or not sums:
            swap(k).wait_recv()
        swap(k).wait_send()
    if sums:
        for k in range(pieces - 1):
            for step in range(3, planes - 1):
                downs[k].advance(step)
            downs[k].finish(down_outs[k])


def middle_of(w_gate, w_up, h_two, d_hidden, middle, out_grad, gain, w_out, q, out, lse, cuts, pieces, planes, shard, width):
    half, model = middle.shape
    rows, units = d_hidden.shape
    columns = q.shape[1]
    heads = columns // width
    chunks, blocks = 4, 4
    dma = pltpu.SemaphoreType.DMA
    staged = [h_two, d_hidden, middle, out_grad, w_out, q, out, lse] + ([] if cuts is None else cuts)
    args = [w_gate, w_up, gain, *staged]
    unit_shape = jax.ShapeDtypeStruct((rows, units), BF16)
    out_shape = [unit_shape] * 4 + [
        jax.ShapeDtypeStruct((rows, model), BF16),
        jax.ShapeDtypeStruct((1, model), F32),
    ]
    out_shape += [jax.ShapeDtypeStruct((heads, rows, 2 * width), BF16)] * 2
    out_shape += [jax.ShapeDtypeStruct((rows, planes * shard), BF16)] * 2
    scratch = Staged.scratch(staged) + Staged.scratch([unit_shape] * 3)
    scratch += [pltpu.VMEM((model, units), BF16)] * 2 + [dma((2 * units // 256,))]
    scratch += [pltpu.VMEM((half, model), F32), pltpu.VMEM((2, rows, model // chunks), F32)]
    scratch += [dma((pieces,))] * 2 + [dma((blocks,))] * 2
    scratch += TensorSum.scratch(chunks, half, model // chunks)
    scratch += Columns.scratch(half, planes * shard)
    if cuts is not None:
        out_shape += [jax.ShapeDtypeStruct((units // pieces, shard), BF16)] * (pieces - 1)
        scratch += LineSum.scratch(planes, (units // pieces, shard)) * (pieces - 1)
    return pl.pallas_call(
        functools.partial(
            middle_kernel,
            planes=planes,
            shard=shard,
            heads=heads,
            width=width,
            pieces=pieces,
            blocks=blocks,
            sums=cuts is not None,
        ),
        out_shape=out_shape,
        in_specs=[ANYWHERE] * 2 + vmem(1) + [ANYWHERE] * len(staged),
        out_specs=[ANYWHERE] * 3 + vmem(len(out_shape) - 3),
        scratch_shapes=scratch,
        compiler_params=pltpu.CompilerParams(
            vmem_limit_bytes=BACK_VMEM_LIMIT, collective_id=2, has_side_effects=True
        ),
        cost_estimate=COST,
        name="middle",
    )(*args)


def through_rope(d_ref, raw_ref, gain, cos, sin, out_ref, width, plain):
    columns = d_ref.shape[1]
    total = jnp.zeros((1, width), F32)
    for at in range(0, columns - plain, width):
        d = d_ref[:, at : at + width]
        c = d * cos - roll_half(d) * sin
        v = raw_ref[:, at : at + width]
        r = lax.rsqrt(jnp.mean(v * v, axis=1, keepdims=True) + EPS)
        n = v * r
        total = total + jnp.sum(c * n, axis=0, keepdims=True)
        gc = gain * c
        out_ref[:, at : at + width] = (r * (gc - n * jnp.mean(n * gc, axis=1, keepdims=True))).astype(BF16)
    if plain:
        out_ref[:, columns - plain :] = d_ref[:, columns - plain :].astype(BF16)
    return total


def front_kernel(*refs, dp_size, planes, shard, chunks, blocks, sums):
    refs = list(refs)

    def take(count):
        out = refs[:count]
        del refs[:count]
        return out

    q_gain, k_gain, attn_gain, mlp_gain_ref, add_array = take(5)
    count = 15 if sums else 11
    arrays = take(count)
    x_grad, gains, dq_ref, dq_came, dkv_ref, dkv_came, one_ref, one_came = take(8)
    if sums:
        w_up_out, w_q_out, w_kv_out = take(3)
    buffers = take(count)
    inputs = Staged(arrays, buffers, *take(1))
    dkv_in, k_raw, cos_ref, sin_ref, dq_in, q_raw, one_all = buffers[:7]
    x_ref, w_q, w_k, w_v = buffers[7:11]
    if sums:
        two_ref, two_came, up_ref, up_came = buffers[11:]
    mine, gain_came, c_ref, add_ref, add_sem = take(5)
    swap_sems, one_sems, gain_sems = take(4), take(2), take(2)
    one_sum_scratch, one_scratch = take(8), take(6)
    half = x_ref.shape[0] // 2
    model = x_ref.shape[1]
    width = model // chunks
    head = cos_ref.shape[1]
    kv_width = w_k.shape[1]

    device = lax.axis_index("dp")
    core, core_peer, y_peer = tensor_peers()
    x_at = device % 2
    x_peer = {"dp": device + 1 - 2 * x_at}
    plane = device // 2
    one = Columns(one_all, one_ref, one_came, one_scratch, x_at, core, x_peer, core_peer, planes, shard)
    bits = [1 << i for i in range(dp_size.bit_length() - 1)]
    dp_peers = [{"dp": device + bit - 2 * bit * ((device // bit) % 2)} for bit in bits]
    gain_peers = [core_peer, y_peer] + dp_peers
    meets = [(peer, True) for peer in gain_peers]
    if sums:
        up_sum, q_sum, kv_sum = (LineSum(take(6), device, plane, planes, True) for _ in range(3))
        meets += [({"dp": device + 2}, plane < planes - 1), ({"dp": device - 2}, plane > 0)]

    mine_rows = rows_of(core, half)
    add_load = pltpu.make_async_copy(add_array.at[mine_rows, :], add_ref, add_sem)
    inputs.start(one_all)
    if sums:
        inputs.start(*buffers[11:])
    inputs.start(*buffers[:6])
    inputs.start(*buffers[7:11])
    add_load.start()
    greet(meets)
    inputs.wait(one_all)
    one.start()
    if sums:
        inputs.wait(*buffers[11:])
        up_sum.fill_rows(two_ref, two_came, up_ref, up_came)
        up_sum.start()
    inputs.wait(*buffers[:6])
    cos, sin = cos_ref[...], sin_ref[...]
    k_total = through_rope(dkv_in, k_raw, k_gain[...], cos, sin, dkv_ref, head, kv_width)
    kv_swap = remote(dkv_ref, dkv_came, swap_sems[0], swap_sems[1], x_peer)
    kv_swap.start()
    q_total = through_rope(dq_in, q_raw, q_gain[...], cos, sin, dq_ref, head, 0)
    q_swap = remote(dq_ref, dq_came, swap_sems[2], swap_sems[3], x_peer)
    q_swap.start()
    inputs.wait(*buffers[7:11])

    one_sum = TensorSum(one_sum_scratch, mine, core, core_peer, y_peer)
    x = x_ref[...].astype(F32)
    r = lax.rsqrt(jnp.mean(x * x, axis=1, keepdims=True) + EPS)
    for i in range(chunks):
        at = slice(i * width, (i + 1) * width)
        part = (
            dot(dq_ref[...], w_q[at, :], NT)
            + dot(dkv_ref[:, :kv_width], w_k[at, :], NT)
            + dot(dkv_ref[:, kv_width:], w_v[at, :], NT)
        )
        one_sum.add(i, part)
        gains[0, :, at] = jnp.sum(part * (x_ref[:, at].astype(F32) * r), axis=0, keepdims=True)
    gains[0, :, model : 2 * model] = mlp_gain_ref[...]
    gains[0, :, 2 * model : 2 * model + head] = q_total
    gains[0, :, 2 * model + head :] = k_total
    one.forward()
    one.store()

    def gain_swap(k):
        return remote(
            gains.at[k], gain_came.at[k], gain_sems[0].at[k], gain_sems[1].at[k], gain_peers[k]
        )

    def gain_add(k):
        gain_swap(k).wait_recv()
        gains[k + 1] = gains[k] + gain_came[k]
        if k + 1 < len(gain_peers):
            gain_swap(k + 1).start()

    gain_swap(0).start()

    def advance(line, step):
        if sums and step <= planes - 2:
            line.advance(step)

    gain_add(0)
    if sums:
        advance(up_sum, 1)
        kv_swap.wait_recv()
        one.over_core().wait_recv()
        kv_sum.fill_rows(one_ref, one_came, dkv_ref, dkv_came)
        kv_sum.start()
    gain_add(1)
    if sums:
        q_swap.wait_recv()
        q_sum.fill_rows(one_ref, one_came, dq_ref, dq_came)
        q_sum.start()
        advance(up_sum, 2)
    gain_add(2)

    def give(out, sems):
        rows = out.at[mine_rows, :]
        return remote(rows, rows, sems[0], sems[1], core_peer)

    for i in range(chunks):
        c_ref[:, i * width : (i + 1) * width] = one_sum.total(i)
    add_load.wait()
    step = half // blocks
    for b in range(blocks):
        at = slice(b * step, (b + 1) * step)
        whole_at = pl.ds(pl.multiple_of(core * half + b * step, step), step)
        v = x_ref[whole_at, :].astype(F32)
        v_r = lax.rsqrt(jnp.mean(v * v, axis=1, keepdims=True) + EPS)
        n = v * v_r
        gc = c_ref[at, :] * attn_gain[...]
        d = v_r * (gc - n * jnp.mean(n * gc, axis=1, keepdims=True))
        x_grad[whole_at, :] = (d + add_ref[at, :].astype(F32)).astype(BF16)
    give(x_grad, one_sems).start()
    for k in range(3, len(gain_peers)):
        gain_add(k)
    if sums:
        advance(kv_sum, 1)
        advance(q_sum, 1)
    if sums:
        advance(kv_sum, 2)
        advance(q_sum, 2)
        for line in (up_sum, kv_sum, q_sum):
            for step in range(3, planes - 1):
                advance(line, step)
        up_sum.finish(w_up_out)
        kv_sum.finish(w_kv_out)
        q_sum.finish(w_q_out)
    else:
        kv_swap.wait_recv()
        q_swap.wait_recv()
        one.over_core().wait_recv()
    one.over_x().wait_send()
    one.over_core().wait_send()
    kv_swap.wait_send()
    q_swap.wait_send()
    give(x_grad, one_sems).wait_recv()
    give(x_grad, one_sems).wait_send()
    for k in range(len(gain_peers)):
        gain_swap(k).wait_send()
    one_sum.finish()


def front(dq, dkv, q_raw, k_raw, q_gain, k_gain, cos, sin, h_one, weights, x, d_attn, attn_gain, mlp_gain, grads, dp_size, shard):
    rows, model = x.shape
    half = rows // 2
    planes = dp_size // 2
    chunks = 4
    width = model // chunks
    stages = dp_size.bit_length() + 1
    dma = pltpu.SemaphoreType.DMA
    gains = (2 * model + 2 * cos.shape[1],)
    staged = [dkv, k_raw, cos, sin, dq, q_raw, h_one, x, *weights]
    if grads is not None:
        staged += grads
    args = [q_gain, k_gain, attn_gain, mlp_gain, d_attn, *staged]
    cut_shape = jax.ShapeDtypeStruct((rows, planes * shard), BF16)
    whole = jax.ShapeDtypeStruct((rows, model), BF16)
    q_shape, kv_shape = jax.ShapeDtypeStruct(dq.shape, BF16), jax.ShapeDtypeStruct(dkv.shape, BF16)
    out_shape = [whole, jax.ShapeDtypeStruct((stages + 1, 1) + gains, F32)]
    out_shape += [q_shape, q_shape, kv_shape, kv_shape, cut_shape, cut_shape]
    scratch = Staged.scratch(staged)
    scratch += [pltpu.VMEM((2, rows, width), F32)]
    scratch += [pltpu.VMEM((stages, 1) + gains, F32), pltpu.VMEM((half, model), F32)]
    scratch += [pltpu.VMEM((half, model), BF16), dma]
    scratch += [dma] * 6 + [dma((stages,))] * 2
    scratch += TensorSum.scratch(chunks, half, width)
    scratch += Columns.scratch(half, planes * shard)
    if grads is not None:
        for columns in (grads[2].shape[1], dq.shape[1], dkv.shape[1]):
            out_shape.append(jax.ShapeDtypeStruct((shard, columns), BF16))
            scratch += LineSum.scratch(planes, (shard, columns))
    return pl.pallas_call(
        functools.partial(
            front_kernel,
            dp_size=dp_size,
            planes=planes,
            shard=shard,
            chunks=chunks,
            blocks=4,
            sums=grads is not None,
        ),
        out_shape=out_shape,
        in_specs=vmem(4) + [ANYWHERE] * (len(args) - 4),
        out_specs=vmem(len(out_shape)),
        scratch_shapes=scratch,
        compiler_params=pltpu.CompilerParams(
            vmem_limit_bytes=BACK_VMEM_LIMIT, collective_id=3, has_side_effects=True
        ),
        cost_estimate=COST,
        name="front",
    )(*args)


def widen_kernel(*refs, results, gains):
    refs = list(refs)

    def take(count):
        out = refs[:count]
        del refs[:count]
        return out

    count = 1 + max(i for parts in results for i, _ in parts)
    block_in = take(1)[0]
    arrays = take(count)
    if gains:
        gain_ref = take(1)[0]
    block_out = take(1)[0]
    outs = take(len(results))
    if gains:
        attn_out, mlp_out, q_out, k_out = take(4)
    buffers = take(count)
    inputs = Staged(arrays, buffers, *take(1))
    out_buffers = take(len(results))
    outputs = Staged(outs, out_buffers, *take(1), out=True)
    block, block_sems = take(2)
    block_load = pltpu.make_async_copy(block_in, block, block_sems.at[0])
    block_copy = pltpu.make_async_copy(block, block_out, block_sems.at[1])
    block_load.start()
    inputs.start()
    if gains:
        shard, head = attn_out.shape[1], q_out.shape[1]
        model = (gain_ref.shape[1] - 2 * head) // 2
        at = pl.multiple_of(lax.axis_index("dp") * shard, shard)
        attn_out[...] = gain_ref[:, pl.ds(at, shard)]
        mlp_out[...] = gain_ref[:, pl.ds(pl.multiple_of(model + at, shard), shard)]
        q_out[...] = gain_ref[:, 2 * model : 2 * model + head]
        k_out[...] = gain_ref[:, 2 * model + head :]
    block_load.wait()
    block_copy.start()
    waited = set()
    for parts, out in zip(results, out_buffers):
        row = 0
        for i, column in parts:
            part = buffers[i]
            if i not in waited:
                inputs.wait(part)
                waited.add(i)
            height = part.shape[0]
            out[row : row + height, :] = part[:, column : column + out.shape[1]].astype(F32)
            row += height
        outputs.start(out)
    block_copy.wait()
    outputs.wait()


def widen(block_out, arrays, results, shapes, gains, shard, head):
    out_shape = [jax.ShapeDtypeStruct(block_out.shape, BF16)]
    out_shape += [jax.ShapeDtypeStruct(s, F32) for s in shapes]
    args = [block_out, *arrays]
    rows = [] if gains is None else [(1, shard), (1, shard), (1, head), (1, head)]
    if gains is not None:
        args.append(gains)
    return pl.pallas_call(
        functools.partial(widen_kernel, results=results, gains=gains is not None),
        out_shape=out_shape + [jax.ShapeDtypeStruct(s, F32) for s in rows],
        in_specs=[ANYWHERE] * (1 + len(arrays)) + vmem(0 if gains is None else 1),
        out_specs=[ANYWHERE] * (1 + len(shapes)) + vmem(len(rows)),
        scratch_shapes=Staged.scratch(arrays)
        + Staged.scratch(out_shape[1:])
        + [pltpu.VMEM(block_out.shape, BF16), pltpu.SemaphoreType.DMA((2,))],
        compiler_params=params(),
        cost_estimate=COST,
        name="widen",
    )(*args)


class Chain:
    def __init__(self):
        self.last = None

    def mark(self, value):
        self.last = value

    def __call__(self, *values):
        if self.last is None:
            return values
        return lax.optimization_barrier((*values, self.last))[:-1]


class ZSum:
    def __init__(self, part, dim, shard, planes, z_at):
        self.part, self.dim, self.shard, self.planes, self.z_at = part, dim, shard, planes, z_at
        self.at = 0
        self.came = None

    def term(self, j):
        j = jnp.clip(j, 0, self.planes - 1)
        return lax.dynamic_slice_in_dim(self.part, j * self.shard, self.shard, self.dim)

    def send(self, up, down):
        last = self.planes - 1
        self.at += 1
        up_pairs = [(2 * z + x, 2 * z + 2 + x) for z in range(last) for x in range(2) if z < self.at]
        down_pairs = [
            (2 * (last - z) + x, 2 * (last - 1 - z) + x)
            for z in range(last)
            for x in range(2)
            if z < self.at
        ]
        self.came = lax.ppermute(up, "dp", up_pairs), lax.ppermute(down, "dp", down_pairs)

    def terms(self):
        planes, z_at, at = self.planes, self.z_at, self.at
        return self.term(planes - 1 - at + z_at), self.term(at + 1 - planes + z_at)

    def start(self):
        self.send(*self.terms())

    def step(self, chain):
        if self.at >= self.planes - 1:
            return
        up, down = chain(*self.came)
        up_term, down_term = self.terms()
        up, down = up + up_term, down + down_term
        chain.mark(up)
        self.send(up, down)

    def finish(self, chain):
        if self.at == 0:
            self.start()
        while self.at < self.planes - 1:
            self.step(chain)
        up, down = chain(*self.came)
        total = self.term(self.z_at).astype(F32) + up.astype(F32) + down.astype(F32)
        chain.mark(total)
        return total


def shards(
    dp_size,
    tensor_size,
    tokens,
    norm_attn,
    w_query,
    key_weight,
    value_weight,
    query_gain,
    key_gain,
    w_out,
    norm_mlp,
    w_gate,
    w_up,
    w_down,
    out_grad,
    prefix_len,
):
    rows, model = tokens.shape
    width = query_gain.shape[0]
    kv_heads = key_weight.shape[1] // width
    repeat = w_query.shape[1] // key_weight.shape[1]
    dims = (kv_heads, repeat, width)
    group = dp_size // prefix_len.shape[0]
    planes = dp_size // 2
    group_planes = group // 2
    half = rows // 2
    shard = model // dp_size
    assert tensor_size == 4 and MAX_PREFIX <= 4 * rows

    device = lax.axis_index("dp")
    x_at = device % 2
    z_at = device // 2
    sequence = device // group
    member = device % group
    plane = member // 2
    prefix = jnp.sum(jnp.where(jnp.arange(prefix_len.shape[0]) == sequence, prefix_len, 0))

    x_pairs = [(d, d ^ 1) for d in range(dp_size)]

    def x_swap(value):
        return lax.ppermute(value, "dp", x_pairs)

    positions = (member * rows + jnp.arange(rows)).astype(F32)
    counter = jnp.arange(width // 2, dtype=F32)
    angles = positions[:, None] * (ROPE_BASE ** (-2.0 * counter / width))[None, :]
    cos, sin = jnp.cos(angles), jnp.sin(angles)
    cos = jnp.concatenate([cos, cos], axis=1)
    sin = jnp.concatenate([-sin, sin], axis=1)
    norm_attn_row = norm_attn[None, :]
    norm_mlp_row = norm_mlp[None, :]
    q_gain_row = query_gain[None, :]
    k_gain_row = key_gain[None, :]

    prefix_at = prefix[None].astype(jnp.int32)
    heads_b, lse, kv_all, h_one, q, q_raw, k_raw = attn_fwd(
        prefix_at,
        tokens,
        norm_attn_row,
        w_query,
        key_weight,
        value_weight,
        q_gain_row,
        k_gain_row,
        cos,
        sin,
        group,
        dims,
    )
    fused = planes == group_planes and shard % 128 == 0
    pieces = 3
    middle, h_two, d_hidden, og_keep, og_came, heads_came = attention_out(
        heads_b, w_out, tokens, norm_mlp_row, out_grad, w_down, planes, shard
    )
    outs = middle_of(
        w_gate,
        w_up,
        h_two,
        d_hidden,
        middle,
        out_grad,
        norm_mlp_row,
        w_out,
        q,
        heads_b,
        lse,
        [og_keep, og_came] if fused else None,
        pieces,
        planes,
        shard,
        width,
    )
    hidden, d_gate, d_up, hidden_came, d_attn, norm_mlp_part, qx, dox, h_two_keep, h_two_came = outs[:10]

    grads = None
    if fused:
        grads = [hidden_came, og_keep, og_came, d_gate, h_two_keep, h_two_came]
        grads += [heads_b, heads_came]
        w_down_parts = outs[10:]
    shared = [d_attn, d_up, hidden, w_down, middle]
    outs = back(prefix_at, qx, dox, kv_all, shared, grads, group, planes, shard, pieces, dims)
    dq, kv_grad, d_attn_keep, d_attn_came, up_came, block_out = outs[:6]
    chain = Chain()
    chain.mark(dq)
    if fused:
        w_down_parts = [*w_down_parts, outs[6]]
        w_gate_grad, w_out_grad = outs[7:]
    else:
        down_part = (dot(hidden, og_keep, TN) + dot(hidden_came, og_came, TN)).astype(BF16)
        w_down_grad = ZSum(down_part, 1, shard, planes, z_at).finish(chain)
        gate_part = dot(h_two_keep, d_gate, TN) + dot(h_two_came, x_swap(d_gate), TN)
        w_gate_grad = ZSum(gate_part.astype(BF16), 0, shard, planes, z_at).finish(chain)
        out_part = dot(heads_b, d_attn_keep, TN) + dot(heads_came, d_attn_came, TN)
        w_out_grad = ZSum(out_part.astype(BF16), 1, shard, planes, z_at).finish(chain)

    up_grads = [h_two_keep, h_two_came, d_up, up_came] if fused else None
    outs = front(
        *chain(dq),
        kv_grad,
        q_raw,
        k_raw,
        q_gain_row,
        k_gain_row,
        cos,
        sin,
        h_one,
        (w_query, key_weight, value_weight),
        tokens,
        d_attn,
        norm_attn_row,
        0.5 * norm_mlp_part,
        up_grads,
        dp_size,
        shard,
    )
    tokens_grad, gains, dq_b, dq_came, dkv_b, dkv_came, h_one_keep, h_one_came = outs[:8]
    if fused:
        w_up_grad, w_query_grad, w_kv_grad = outs[8:]
    else:
        chain.mark(tokens_grad)

        def by_rows(left, left_came, right, right_came):
            part = dot(left, right, TN) + dot(left_came, right_came, TN)
            return ZSum(part.astype(BF16), 0, shard, planes, z_at).finish(chain)

        w_up_grad = by_rows(h_two_keep, h_two_came, d_up, up_came)
        w_query_grad = by_rows(h_one_keep, h_one_came, dq_b, dq_came)
        w_kv_grad = by_rows(h_one_keep, h_one_came, dkv_b, dkv_came)
    kv_width = kv_heads * width
    if fused:
        arrays = [w_gate_grad, w_out_grad, *w_down_parts, w_up_grad, w_query_grad, w_kv_grad, tokens_grad]
        n = 2 + len(w_down_parts)
        results = [[(0, 0)], [(1, 0)], [(i, 0) for i in range(2, n)]]
        results += [[(n, 0)], [(n + 1, 0)], [(n + 2, 0)], [(n + 2, kv_width)], [(n + 3, 0)]]
        units = w_gate.shape[1]
        columns = w_query.shape[1]
        shapes = [(shard, units), (columns, shard), (units, shard), (shard, units), (shard, columns)]
        shapes += [(shard, kv_width)] * 2 + [(rows, model)]
        outs = widen(block_out, arrays, results, shapes, gains[-1], shard, width)
        block_out, w_gate_grad, w_out_grad, w_down_grad, w_up_grad, w_query_grad = outs[:6]
        w_key_grad, w_value_grad, tokens_grad = outs[6:9]
        norm_attn_grad, norm_mlp_grad, query_gain_grad, key_gain_grad = (v[0] for v in outs[9:])
    else:
        w_key_grad, w_value_grad = w_kv_grad[:, :kv_width], w_kv_grad[:, kv_width:]
        tokens_grad = tokens_grad.astype(F32)
        gains = gains[-1, 0]
        norm_attn_grad = lax.dynamic_slice_in_dim(gains, device * shard, shard, 0)
        norm_mlp_grad = lax.dynamic_slice_in_dim(gains, model + device * shard, shard, 0)
        query_gain_grad, key_gain_grad = gains[2 * model : 2 * model + width], gains[2 * model + width :]
    return (
        block_out,
        tokens_grad,
        norm_attn_grad,
        w_query_grad,
        w_key_grad,
        w_value_grad,
        query_gain_grad,
        key_gain_grad,
        w_out_grad,
        norm_mlp_grad,
        w_gate_grad,
        w_up_grad,
        w_down_grad,
    )


def solution(mesh):
    placed = (
        P("dp", None),
        P(),
        P(None, "tensor"),
        P(None, "tensor"),
        P(None, "tensor"),
        P(),
        P(),
        P("tensor", None),
        P(),
        P(None, "tensor"),
        P(None, "tensor"),
        P("tensor", None),
        P("dp", None),
        P(),
    )
    return jax.shard_map(
        functools.partial(shards, mesh.shape["dp"], mesh.shape["tensor"]),
        mesh=mesh,
        in_specs=placed,
        out_specs=(
            P("dp", None),
            P("dp", None),
            P("dp"),
            P("dp", "tensor"),
            P("dp", "tensor"),
            P("dp", "tensor"),
            P(),
            P(),
            P("tensor", "dp"),
            P("dp"),
            P("dp", "tensor"),
            P("dp", "tensor"),
            P("tensor", "dp"),
        ),
        check_vma=False,
    )
```

profile of v0, /device:TPU:0, one launch (start us, length us, event | category | flops | bytes accessed | tf_op | source)
XLA Modules:
  0.0 414.6 jit_solution(13516068969763907824)
XLA Ops:
  1.3 1.0 fusion
  2.3 1.0 pad_maximum_fusion
  3.3 36.9 %attn_fwd.1 = (bf16[512,512]{1,0:T(8,128)(2,1)}, f32[512,512]{1,0:T(8,128)}, bf16[8,512,512]{2,1,0:T(8,128)(2,1)}, bf16[512,2048]{1,0:T(8,128)(2,1)}, bf16[512,5...) custom-call(s32[1]{0:T(128)S(6)} %select_n.16.refs_0_, f32[1,2048]{1,0:T(1,128)} %bitcast.11, ...), custom_call_target="tpu_custom_call" | custom-call | flops 1000 | bytes 1000 | tf_op jit(solution)/shard_map/attn_fwd/pallas_call | solution.py:549
  40.3 36.9 %attention_out.1 = (f32[256,2048]{1,0:T(8,128)}, bf16[512,2048]{1,0:T(8,128)(2,1)}, f32[512,1536]{1,0:T(8,128)}, bf16[512,1024]{1,0:T(8,128)(2,1)}, bf16[512,1024]{1,0:T(8,128)(2,1)}, /*index=5*/bf16[512,512]{1,0:T(8,128)(2,1)}) custom-call(bf16[512,512]{1,0:T(8,128)(2,1)} %get-tuple-element.63.refs_0_.refs_9_.refs_15_, bf16[512,2048]{1,0:T(8,128)(2,1)} %refs_7_.1, ...), custom_call_target="tpu_custom_call" | custom-call | flops 1000 | bytes 1000 | tf_op jit(solution)/shard_map/attention_out/pallas_call | solution.py:1067
  77.2 90.6 %middle.1 = (bf16[512,1536]{1,0:T(8,128)(2,1)}, bf16[512,1536]{1,0:T(8,128)(2,1)}, bf16[512,1536]{1,0:T(8,128)(2,1)}, bf16[512,1536]{1,0:T(8,128)(2,1)}, bf16[51...) custom-call(bf16[2048,1536]{1,0:T(8,128)(2,1)} %refs_0_.1, ...), custom_call_target="tpu_custom_call" | custom-call | flops 1000 | bytes 1000 | tf_op jit(solution)/shard_map/middle/pallas_call | solution.py:1289
  167.8 0.0 copy-start
  167.8 140.7 %back.1 = (f32[512,512]{1,0:T(8,128)}, f32[512,512]{1,0:T(8,128)}, bf16[512,1024]{1,0:T(8,128)(2,1)}, bf16[512,1024]{1,0:T(8,128)(2,1)}, bf16[512,1536]{1,0:T(8,...) custom-call(s32[1]{0:T(128)S(6)} %select_n.16.refs_0_, ...), custom_call_target="tpu_custom_call" | custom-call | flops 1000 | bytes 1000 | tf_op jit(solution)/shard_map/back/pallas_call | solution.py:950
  308.5 0.0 copy-done
  308.5 0.6 broadcast_multiply_fusion.refs_3_
  309.1 95.0 %front.1 = (bf16[512,2048]{1,0:T(8,128)(2,1)}, f32[6,1,4352]{2,1,0:T(1,128)}, bf16[512,512]{1,0:T(8,128)(2,1)}, bf16[512,512]{1,0:T(8,128)(2,1)}, bf16[512,512]{...) custom-call(f32[1,128]{1,0:T(1,128)} %bitcast.16, ...), custom_call_target="tpu_custom_call" | custom-call | flops 1000 | bytes 1000 | tf_op jit(solution)/shard_map/front/pallas_call | solution.py:1523
  404.2 1.3 slice_bitcast_fusion.refs_10_
  405.5 8.7 %widen.1 = (bf16[512,2048]{1,0:T(8,128)(2,1)}, f32[256,1536]{1,0:T(8,128)}, f32[512,256]{1,0:T(8,128)}, f32[1536,256]{1,0:T(8,128)}, f32[256,1536]{1,0:T(8,128)}...) custom-call(bf16[512,2048]{1,0:T(8,128)(2,1)} %get-tuple-element.82., ...), custom_call_target="tpu_custom_call" | custom-call | flops 1000 | bytes 1000 | tf_op jit(solution)/shard_map/widen/pallas_call | solution.py:1604
  (2 shorter events, 0.0 us)
Async XLA Ops:
  167.8 140.8 %copy-start = (f32[1,2048]{1,0:T(1,128)S(1)}, f32[1,2048]{1,0:T(1,128)}, u32[]{:S(2)}) copy-start(f32[1,2048]{1,0:T(1,128)} %get-tuple-element.88) | copy-start | bytes 24580
where the time goes:
time: 423 us; the launch traced here: 415 us
  Pallas kernels  409 us (97%)
    pallas_call x1, Pallas kernels, back(): pl.pallas_call(functools.partial(back_kernel, group=group, planes=planes,...  141 us
    pallas_call x1, Pallas kernels, front(): pl.pallas_call(functools.partial(front_kernel, dp_size=dp_size, planes=pl...  95 us
    pallas_call x1, Pallas kernels, middle_of(): pl.pallas_call(functools.partial(middle_kernel, planes=planes, shard=shar...  90.6 us
    pallas_call x1, Pallas kernels, attn_fwd(): pl.pallas_call(functools.partial(attn_fwd_kernel, group=group, kv_heads=k...  36.9 us
    pallas_call x1, Pallas kernels, attention_out(): pl.pallas_call(functools.partial(out_kernel, planes=planes, shard=shard,...  36.9 us
    pallas_call x1, Pallas kernels, widen(): pl.pallas_call(functools.partial(widen_kernel, results=results, gains=gai...  8.66 us

commit v1 on v0

--- a/solution.py
+++ b/solution.py
@@ -3,6 +3,7 @@
 
 import jax
 import jax.numpy as jnp
+import numpy as np
 from jax import lax
 from jax.experimental import pallas as pl
 from jax.experimental.pallas import tpu as pltpu
@@ -86,6 +87,11 @@
 
 
 ANYWHERE = pl.BlockSpec(memory_space=pl.ANY)
+
+
+def table_rows(tables, member, rows):
+    at = pl.ds(pl.multiple_of(member * rows, rows), rows)
+    return [t.at[at, :] for t in tables]
 
 
 def tensor_peers():
@@ -335,6 +341,8 @@
 
     prefix_ref, gain_ref, q_gain, k_gain = take(4)
     arrays = take(6)
+    member = lax.axis_index("dp") % group
+    arrays[3:5] = table_rows(arrays[3:5], member, arrays[0].shape[0])
     o_ref, lse_ref, all_out = take(3)
     outs = take(4)
     buffers = take(6)
@@ -343,7 +351,8 @@
     out_buffers = take(4)
     h_ref, q_ref, q_raw, k_raw = out_buffers
     outputs = Staged(outs, out_buffers, *take(1), out=True)
-    kv_ref, all_ref, all_sems, acc, send_x, recv_x, send_z, recv_z, send_down = take(9)
+    kv_ref, all_ref, all_sems, acc, send_x, recv_x, send_z, recv_z = take(8)
+    send_down, send_rest, recv_rest = take(3)
     rows = q_ref.shape[0]
     kv_width = kv_heads * width
     planes = group // 2
@@ -363,10 +372,14 @@
     def source(slot):
         return kv_ref if slot == 0 else all_ref.at[2 * slot]
 
+    split = planes - 1 if planes > 2 else planes
+    upper = pl.ds(rows // 2, rows - rows // 2)
+
     def to_x(slot):
+        part = pl.ds(0, rows // 2 if slot == split else rows)
         return pltpu.make_async_remote_copy(
-            src_ref=source(slot),
-            dst_ref=all_ref.at[2 * slot + 1],
+            src_ref=source(slot).at[part, :],
+            dst_ref=all_ref.at[2 * slot + 1, part, :],
             send_sem=send_x.at[slot],
             recv_sem=recv_x.at[slot],
             device_id={"dp": x_other},
@@ -381,6 +394,15 @@
             recv_sem=recv_z.at[slot],
             device_id={"dp": device + 2},
             device_id_type=pl.DeviceIdType.MESH,
+        )
+
+    def rest_to_z():
+        return remote(
+            all_ref.at[2 * split - 1, upper, :],
+            all_ref.at[2 * split + 1, upper, :],
+            send_rest,
+            recv_rest,
+            {"dp": device + 2},
         )
 
     def to_first():
@@ -482,6 +504,14 @@
             else:
                 work(all_ref.at[2 * slot], there + x_at, False)
             to_x(slot).wait_recv()
+            if slot == split - 1:
+
+                @pl.when(plane == split - 1)
+                def _():
+                    rest_to_z().start()
+
+            if slot == split:
+                rest_to_z().wait_recv()
             store(2 * slot + 1).start()
             if slot == 1:
 
@@ -506,6 +536,8 @@
         lse_ref[:, head * width : (head + 1) * width] = jnp.log2(total) * (1.0 / coef)
 
     outputs.wait()
+    if split < planes:
+        pl.when(plane == split - 1)(lambda: rest_to_z().wait_send())
     to_x(0).wait_send()
     for slot in range(planes):
 
@@ -540,6 +572,7 @@
     dma = pltpu.SemaphoreType.DMA
     block = (rows, 2 * kv_heads * width)
     staged = [x, key_weight, value_weight, cos, sin, w_query]
+    table = jax.ShapeDtypeStruct((rows, width), F32)
     early = [
         jax.ShapeDtypeStruct(x.shape, BF16),
         jax.ShapeDtypeStruct((rows, columns), BF16),
@@ -564,12 +597,12 @@
         + early,
         in_specs=[smem()] + vmem(3) + [ANYWHERE] * 6,
         out_specs=vmem(2) + [ANYWHERE] * 5,
-        scratch_shapes=Staged.scratch(staged)
+        scratch_shapes=Staged.scratch([x, key_weight, value_weight, table, table, w_query])
         + Staged.scratch(early)
         + [pltpu.VMEM(block, BF16), pltpu.VMEM((group,) + block, BF16), dma((group,))]
         + [pltpu.VMEM((heads, rows, 2 * width), F32)]
         + [dma((planes,))] * 4
-        + [dma],
+        + [dma] * 3,
         compiler_params=pltpu.CompilerParams(
             vmem_limit_bytes=VMEM_LIMIT, collective_id=0, has_side_effects=True
         ),
@@ -992,15 +1025,15 @@
     heads_ref, w_ref, og_ref, x_ref = buffers
     inputs = Staged(arrays, buffers, *take(1))
     d_hidden_ref, d_hidden_sem = take(2)
-    down_buf, down_sems, mine_ref, h_send, h_recv, heads_send, heads_recv = take(7)
+    down_buf, down_sems, whole_ref, h_send, h_recv, heads_send, heads_recv = take(7)
     scratch = refs
     device = lax.axis_index("dp")
     core, core_peer, y_peer = tensor_peers()
     x_at = device % 2
     x_peer = {"dp": device + 1 - 2 * x_at}
     half = middle_ref.shape[0]
-    total = TensorSum(scratch[:8], mine_ref, core, core_peer, y_peer)
-    chunks, width = total.chunks, total.width
+    total = TensorSum(scratch[:8], None, core, core_peer, y_peer)
+    step = half // blocks
     place = (x_at, core, x_peer, core_peer, planes, shard)
     og = Columns(og_ref, og_keep, og_came, scratch[8:14], *place)
     tiles = down_sems.shape[0]
@@ -1017,8 +1050,19 @@
     heads_swap = remote(heads_ref, heads_came, heads_send, heads_recv, x_peer)
     inputs.wait(heads_ref, w_ref)
     heads_swap.start()
-    for i in range(chunks):
-        total.add(i, dot(heads_ref[...], w_ref[:, i * width : (i + 1) * width]))
+
+    def rows_at(which, b):
+        return pl.ds(pl.multiple_of(which * half + b * step, step), step)
+
+    whole_ref[...] = dot(heads_ref[...], w_ref[...])
+    for b in range(blocks):
+        total.away[b] = whole_ref[rows_at(1 - core, b), :].astype(BF16)
+        total.over_core(b).start()
+    for b in range(blocks):
+        total.over_core(b).wait_recv()
+        mine = whole_ref[rows_at(core, b), :] + total.core_came[b].astype(F32)
+        total.both[b] = mine.astype(BF16)
+        total.over_y(b).start()
     inputs.wait(og_ref)
     og.start()
     og.store()
@@ -1028,21 +1072,17 @@
         d_hidden_ref[:, at] = dot(og_ref[...], down_buf[at, :], NT)
     d_hidden_copy = pltpu.make_async_copy(d_hidden_ref, d_hidden_out, d_hidden_sem)
     d_hidden_copy.start()
-    mine = rows_of(core, half)
     inputs.wait(x_ref)
-    for i in range(chunks):
-        at = slice(i * width, (i + 1) * width)
-        middle_ref[:, at] = x_ref[mine, at].astype(F32) + total.total(i)
-    step = half // blocks
 
     def to_core(b):
-        rows = h_ref.at[pl.ds(pl.multiple_of(core * half + b * step, step), step), :]
+        rows = h_ref.at[rows_at(core, b), :]
         return remote(rows, rows, h_send.at[b], h_recv.at[b], core_peer)
 
     for b in range(blocks):
-        v = middle_ref[b * step : (b + 1) * step, :]
+        at = rows_at(core, b)
+        v = x_ref[at, :].astype(F32) + total.total(b)
+        middle_ref[b * step : (b + 1) * step, :] = v
         r = lax.rsqrt(jnp.mean(v * v, axis=1, keepdims=True) + EPS)
-        at = pl.ds(pl.multiple_of(core * half + b * step, step), step)
         h_ref[at, :] = (v * r * gain_ref[...]).astype(BF16)
         to_core(b).start()
     og.forward()
@@ -1060,7 +1100,7 @@
     rows, model = x.shape
     half = rows // 2
     units = w_down.shape[0]
-    chunks, blocks = 4, 4
+    blocks = 4
     tiles = units // math.gcd(units, 256)
     dma = pltpu.SemaphoreType.DMA
     cut_shape = jax.ShapeDtypeStruct((rows, planes * shard), BF16)
@@ -1078,8 +1118,8 @@
         scratch_shapes=Staged.scratch([heads, w_out, out_grad, x])
         + [pltpu.VMEM((rows, units), F32), dma]
         + [pltpu.VMEM((units, model), BF16), dma((tiles,))]
-        + [pltpu.VMEM((2, rows, model // chunks), F32), dma((blocks,)), dma((blocks,)), dma, dma]
-        + TensorSum.scratch(chunks, half, model // chunks)
+        + [pltpu.VMEM((rows, model), F32), dma((blocks,)), dma((blocks,)), dma, dma]
+        + TensorSum.scratch(blocks, half // blocks, model)
         + Columns.scratch(half, planes * shard),
         compiler_params=pltpu.CompilerParams(
             vmem_limit_bytes=VMEM_LIMIT, collective_id=4, has_side_effects=True
@@ -1162,7 +1202,7 @@
         at = slice(t * tile, (t + 1) * tile)
         gate = dot(h_ref[...], gate_buf[:, at])
         up = dot(h_ref[...], up_buf[:, at])
-        sig = 1.0 / (1.0 + jnp.exp(-gate))
+        sig = 0.5 * jnp.tanh(0.5 * gate) + 0.5
         silu = gate * sig
         d = d_ref[:, at]
         hid_ref[:, at] = (silu * up).astype(BF16)
@@ -1188,13 +1228,13 @@
     for i in range(chunks):
         at = slice(i * columns, (i + 1) * columns)
         total.add(i, dot(gate_ref[...], gate_buf[at, :], NT) + dot(up_ref[...], up_buf[at, :], NT))
-        if i == chunks - 2:
+        if i == chunks // 2:
             down_start(0)
     for i in range(chunks):
-        if i == 1:
+        if i == chunks // 4:
             down_start(1)
             h_two.start()
-        if i == 2:
+        if i == chunks // 2:
             down_advance(0, 1)
         c_ref[:, i * columns : (i + 1) * columns] = total.total(i)
     down_advance(0, 2)
@@ -1326,7 +1366,7 @@
     return total
 
 
-def front_kernel(*refs, dp_size, planes, shard, chunks, blocks, sums):
+def front_kernel(*refs, dp_size, group, planes, shard, chunks, blocks, sums):
     refs = list(refs)
 
     def take(count):
@@ -1337,6 +1377,7 @@
     q_gain, k_gain, attn_gain, mlp_gain_ref, add_array = take(5)
     count = 15 if sums else 11
     arrays = take(count)
+    arrays[2:4] = table_rows(arrays[2:4], lax.axis_index("dp") % group, arrays[0].shape[0])
     x_grad, gains, dq_ref, dq_came, dkv_ref, dkv_came, one_ref, one_came = take(8)
     if sums:
         w_up_out, w_q_out, w_kv_out = take(3)
@@ -1491,7 +1532,7 @@
     one_sum.finish()
 
 
-def front(dq, dkv, q_raw, k_raw, q_gain, k_gain, cos, sin, h_one, weights, x, d_attn, attn_gain, mlp_gain, grads, dp_size, shard):
+def front(dq, dkv, q_raw, k_raw, q_gain, k_gain, cos, sin, h_one, weights, x, d_attn, attn_gain, mlp_gain, grads, dp_size, group, shard):
     rows, model = x.shape
     half = rows // 2
     planes = dp_size // 2
@@ -1509,7 +1550,8 @@
     q_shape, kv_shape = jax.ShapeDtypeStruct(dq.shape, BF16), jax.ShapeDtypeStruct(dkv.shape, BF16)
     out_shape = [whole, jax.ShapeDtypeStruct((stages + 1, 1) + gains, F32)]
     out_shape += [q_shape, q_shape, kv_shape, kv_shape, cut_shape, cut_shape]
-    scratch = Staged.scratch(staged)
+    table = jax.ShapeDtypeStruct((rows, cos.shape[1]), F32)
+    scratch = Staged.scratch(staged[:2] + [table, table] + staged[4:])
     scratch += [pltpu.VMEM((2, rows, width), F32)]
     scratch += [pltpu.VMEM((stages, 1) + gains, F32), pltpu.VMEM((half, model), F32)]
     scratch += [pltpu.VMEM((half, model), BF16), dma]
@@ -1524,6 +1566,7 @@
         functools.partial(
             front_kernel,
             dp_size=dp_size,
+            group=group,
             planes=planes,
             shard=shard,
             chunks=chunks,
@@ -1615,6 +1658,14 @@
     )(*args)
 
 
+def rope_tables(length, width):
+    frequency = ROPE_BASE ** (-2.0 * np.arange(width // 2) / width)
+    angles = np.arange(length)[:, None] * frequency[None, :]
+    cos, sin = np.cos(angles), np.sin(angles)
+    tables = np.concatenate([cos, cos], axis=1), np.concatenate([-sin, sin], axis=1)
+    return tuple(jnp.asarray(t.astype(np.float32)) for t in tables)
+
+
 class Chain:
     def __init__(self):
         self.last = None
@@ -1720,12 +1771,7 @@
     def x_swap(value):
         return lax.ppermute(value, "dp", x_pairs)
 
-    positions = (member * rows + jnp.arange(rows)).astype(F32)
-    counter = jnp.arange(width // 2, dtype=F32)
-    angles = positions[:, None] * (ROPE_BASE ** (-2.0 * counter / width))[None, :]
-    cos, sin = jnp.cos(angles), jnp.sin(angles)
-    cos = jnp.concatenate([cos, cos], axis=1)
-    sin = jnp.concatenate([-sin, sin], axis=1)
+    cos, sin = rope_tables(group * rows, width)
     norm_attn_row = norm_attn[None, :]
     norm_mlp_row = norm_mlp[None, :]
     q_gain_row = query_gain[None, :]
@@ -1810,6 +1856,7 @@
         0.5 * norm_mlp_part,
         up_grads,
         dp_size,
+        group,
         shard,
     )
     tokens_grad, gains, dq_b, dq_came, dkv_b, dkv_came, h_one_keep, h_one_came = outs[:8]

time: 423 us -> 414 us (0.979)
  Pallas kernels: 409 us -> 402 us
    pallas_call x1, Pallas kernels: 90.6 us -> 84.9 us  [middle_of(): pl.pallas_call(functools.partial(middle_kernel, planes=planes, shard=shar...]
where the time goes in v1:
time: 414 us; the launch traced here: 405 us
  Pallas kernels  402 us (97%)
    pallas_call x1, Pallas kernels, back(): pl.pallas_call(functools.partial(back_kernel, group=group, planes=planes,...  140 us
    pallas_call x1, Pallas kernels, front(): pl.pallas_call(functools.partial(front_kernel, dp_size=dp_size, group=gro...  95 us
    pallas_call x1, Pallas kernels, middle_of(): pl.pallas_call(functools.partial(middle_kernel, planes=planes, shard=shar...  84.9 us
    pallas_call x1, Pallas kernels, attn_fwd(): pl.pallas_call(functools.partial(attn_fwd_kernel, group=group, kv_heads=k...  37 us
    pallas_call x1, Pallas kernels, attention_out(): pl.pallas_call(functools.partial(out_kernel, planes=planes, shard=shard,...  36.1 us
    pallas_call x1, Pallas kernels, widen(): pl.pallas_call(functools.partial(widen_kernel, results=results, gains=gai...  8.66 us

profile of v1, /device:TPU:0, one launch (start us, length us, event | category | flops | bytes accessed | tf_op | source)
XLA Modules:
  0.0 405.4 jit_solution(14083892495989276321)
XLA Ops:
  1.3 37.0 %attn_fwd.1 = (bf16[512,512]{1,0:T(8,128)(2,1)}, f32[512,512]{1,0:T(8,128)}, bf16[8,512,512]{2,1,0:T(8,128)(2,1)}, bf16[512,2048]{1,0:T(8,128)(2,1)}, bf16[512,5...) custom-call(s32[1]{0:T(128)S(6)} %select_n.10.refs_0_, f32[1,2048]{1,0:T(1,128)} %bitcast.11, ...), custom_call_target="tpu_custom_call" | custom-call | flops 1000 | bytes 1000 | tf_op jit(solution)/shard_map/attn_fwd/pallas_call | solution.py:582
  38.3 36.1 %attention_out.1 = (f32[256,2048]{1,0:T(8,128)}, bf16[512,2048]{1,0:T(8,128)(2,1)}, f32[512,1536]{1,0:T(8,128)}, bf16[512,1024]{1,0:T(8,128)(2,1)}, bf16[512,1024]{1,0:T(8,128)(2,1)}, /*index=5*/bf16[512,512]{1,0:T(8,128)(2,1)}) custom-call(bf16[512,512]{1,0:T(8,128)(2,1)} %get-tuple-element.63.refs_0_.refs_9_.refs_15_, bf16[512,2048]{1,0:T(8,128)(2,1)} %refs_7_.3, ...), custom_call_target="tpu_custom_call" | custom-call | flops 1000 | bytes 1000 | tf_op jit(solution)/shard_map/attention_out/pallas_call | solution.py:1107
  74.4 84.9 %middle.1 = (bf16[512,1536]{1,0:T(8,128)(2,1)}, bf16[512,1536]{1,0:T(8,128)(2,1)}, bf16[512,1536]{1,0:T(8,128)(2,1)}, bf16[512,1536]{1,0:T(8,128)(2,1)}, bf16[51...) custom-call(bf16[2048,1536]{1,0:T(8,128)(2,1)} %refs_0_.1, ...), custom_call_target="tpu_custom_call" | custom-call | flops 1000 | bytes 1000 | tf_op jit(solution)/shard_map/middle/pallas_call | solution.py:1329
  159.3 0.0 copy-start
  159.3 140.1 %back.1 = (f32[512,512]{1,0:T(8,128)}, f32[512,512]{1,0:T(8,128)}, bf16[512,1024]{1,0:T(8,128)(2,1)}, bf16[512,1024]{1,0:T(8,128)(2,1)}, bf16[512,1536]{1,0:T(8,...) custom-call(s32[1]{0:T(128)S(6)} %select_n.10.refs_0_, ...), custom_call_target="tpu_custom_call" | custom-call | flops 1000 | bytes 1000 | tf_op jit(solution)/shard_map/back/pallas_call | solution.py:983
  299.4 0.0 copy-done
  299.4 0.6 broadcast_multiply_fusion.refs_3_
  300.0 95.0 %front.1 = (bf16[512,2048]{1,0:T(8,128)(2,1)}, f32[6,1,4352]{2,1,0:T(1,128)}, bf16[512,512]{1,0:T(8,128)(2,1)}, bf16[512,512]{1,0:T(8,128)(2,1)}, bf16[512,512]{...) custom-call(f32[1,128]{1,0:T(1,128)} %bitcast.16, ...), custom_call_target="tpu_custom_call" | custom-call | flops 1000 | bytes 1000 | tf_op jit(solution)/shard_map/front/pallas_call | solution.py:1565
  395.0 1.3 slice_bitcast_fusion.refs_10_
  396.3 8.7 %widen.1 = (bf16[512,2048]{1,0:T(8,128)(2,1)}, f32[256,1536]{1,0:T(8,128)}, f32[512,256]{1,0:T(8,128)}, f32[1536,256]{1,0:T(8,128)}, f32[256,1536]{1,0:T(8,128)}...) custom-call(bf16[512,2048]{1,0:T(8,128)(2,1)} %get-tuple-element.82., ...), custom_call_target="tpu_custom_call" | custom-call | flops 1000 | bytes 1000 | tf_op jit(solution)/shard_map/widen/pallas_call | solution.py:1647
Async XLA Ops:
  159.3 140.1 %copy-start = (f32[1,2048]{1,0:T(1,128)S(1)}, f32[1,2048]{1,0:T(1,128)}, u32[]{:S(2)}) copy-start(f32[1,2048]{1,0:T(1,128)} %get-tuple-element.88) | copy-start | bytes 24580
